TPU v7x, 32 devices: a whole 2x2x4 slice. The times are simulated.
32 devices in a mesh: seq: 8 (over z, x), head: 4 (over y, core).
Axes of the slice: x: 2, y: 2, z: 4, core: 2. Of those that a mesh axis runs over, the one named last changes fastest.
Arguments:
- tokens: bfloat16 [2048, 3072], P('seq'), may hold values from -16 to 16
- qkv_weight: bfloat16 [3072, 3, 1536], P(None, None, 'head'), may hold values from -1 to 1
- q_gain: float32 [128], replicated, may hold values from 0.5 to 6
- k_gain: float32 [128], replicated, may hold values from 0.5 to 6
- out_weight: bfloat16 [1536, 3072], P('head'), may hold values from -0.15625 to 0.15625
- query_cluster: int32 [12, 2048, 1], P('head', 'seq'), may hold values from 0 to 7; in each aligned block of 256 rows (0 to 255, 256 to 511, ..., all dimensions but the last counted through in order) at most 40 rows name the same one
- key_cluster: int32 [12, 2048, 1], P('head', 'seq'), may hold values from 0 to 31, as said below
- query_slot: int32 [12, 8], P('head'), may hold values from 0 to 7, each once within a row
- key_slot: int32 [12, 32], P('head'), may hold values from 0 to 31, as said below
- pairs: int32 [12, 8, 8], P('head'), may hold values from 0 to 31, as said below
Outputs:
- attention_out: bfloat16 [2048, 3072], P('seq', 'head')
Inputs may be any that keep to these rules, and one draw needn't show every extreme that they name: `query_cluster`: counting the tokens of one device, each query cluster is named at most 40 times in each head. `key_cluster`: in each head, the tokens of one device name 16 key clusters exactly 16 times each and no other; every key cluster is named by exactly 64 tokens in all. Each row is a permutation; query cluster c of head h is owned by index query_slot[h, c] of seq. Each row is a permutation; key cluster c of head h is owned by index key_slot[h, c] // 4 of seq. `pairs`: each list holds 8 key owner slots, exactly one from each range of 4 slots that one index of seq owns, in no particular order.
All inputs are finite; a program needn't handle non-finite values.
Results may differ from a plain program's by a relative error of at most 0.012.
The roundings to bfloat16 on the way count: a program that leaves them out, or rounds other values in their place, can miss the bound.
Values may be sent and summed in bfloat16 or wider, within the bound.
A program may use at most 128 MiB of HBM per device.

v0:
```python
import math

import jax
import jax.numpy as jnp
from jax import lax
from jax.sharding import PartitionSpec as P

KCL_DEV = 4


EPSILON = 1e-06


def normalize(projected, gain):
    mean_square = jnp.mean(projected * projected, axis=-1, keepdims=True)
    return projected * lax.rsqrt(mean_square + EPSILON) * gain


def gather_rows(table, indices):
    return jax.vmap(lambda single, lookup: single[lookup])(table, indices)


def take_rows(source, indices, present):
    picked = gather_rows(source, indices)
    return jnp.where(present[..., None], picked, jnp.zeros((), picked.dtype))


def rank_within(labels):
    length = labels.shape[1]
    positions = jnp.arange(length, dtype=jnp.int32)
    earlier = positions[None, :, None] > positions[None, None, :]
    same_label = labels[:, :, None] == labels[:, None, :]
    return jnp.sum(same_label & earlier, axis=2)


def slot_table(labels, ranks, clusters, depth):
    cluster_ids = jnp.arange(clusters, dtype=jnp.int32)[None, :, None, None]
    rank_ids = jnp.arange(depth, dtype=jnp.int32)[None, None, :, None]
    positions = jnp.arange(labels.shape[1], dtype=jnp.int32)[None, None, None, :]
    matched = (labels[:, None, None, :] == cluster_ids) & (ranks[:, None, None, :] == rank_ids)
    located = jnp.sum(jnp.where(matched, positions, 0), axis=3)
    return (located, jnp.any(matched, axis=3))


def body(
    tokens,
    qkv_weight,
    q_gain,
    k_gain,
    out_weight,
    query_cluster,
    key_cluster,
    query_slot,
    key_slot,
    pairs,
):
    members = lax.axis_size("seq")
    tok_rows = tokens.shape[0]
    heads_here = pairs.shape[0]
    head_width = q_gain.shape[0]
    key_clusters = key_slot.shape[1]
    most_query = max(2, 5 * tok_rows // (4 * members))
    most_key = max(2, 2 * tok_rows // (KCL_DEV * members))
    projected = jnp.dot(
        tokens, qkv_weight.reshape(tokens.shape[1], -1), preferred_element_type=jnp.float32
    )
    projected = projected.reshape(tok_rows, 3, heads_here, head_width).transpose(1, 2, 0, 3)
    queries = normalize(projected[0], q_gain).astype(jnp.bfloat16)
    keys = normalize(projected[1], k_gain).astype(jnp.bfloat16)
    values = projected[2].astype(jnp.bfloat16)
    query_labels = query_cluster[:, :, 0]
    key_labels = key_cluster[:, :, 0]
    query_ranks = rank_within(query_labels)
    key_ranks = rank_within(key_labels)
    query_table, query_present = slot_table(query_labels, query_ranks, members, most_query)
    key_table, key_present = slot_table(key_labels, key_ranks, key_clusters, most_key)
    owner_cluster = jnp.argsort(query_slot, axis=1)
    cluster_of_slot = jnp.argsort(key_slot, axis=1)
    send_index = gather_rows(query_table, owner_cluster).reshape(heads_here, -1)
    send_present = gather_rows(query_present, owner_cluster).reshape(heads_here, -1)
    query_send = take_rows(queries, send_index, send_present)
    owner_lists = gather_rows(cluster_of_slot, pairs.reshape(heads_here, -1))
    query_rows = lax.all_to_all(query_send, "seq", split_axis=1, concat_axis=1, tiled=True)
    direct_index = gather_rows(key_table, owner_lists).reshape(heads_here, -1)
    direct_present = gather_rows(key_present, owner_lists).reshape(heads_here, -1)
    direct_keys = take_rows(keys, direct_index, direct_present)
    direct_values = take_rows(values, direct_index, direct_present)
    direct_flags = direct_present.astype(jnp.bfloat16)
    key_block, value_block, key_flags = (
        lax.all_to_all(direct_keys, "seq", split_axis=1, concat_axis=1, tiled=True),
        lax.all_to_all(direct_values, "seq", split_axis=1, concat_axis=1, tiled=True),
        lax.all_to_all(direct_flags, "seq", split_axis=1, concat_axis=1, tiled=True),
    )
    inverse_root = 1.0 / math.sqrt(head_width)

    def attend(operands):
        query_block, block_keys, block_values, block_flags = operands
        scores = (
            lax.dot_general(
                query_block,
                block_keys,
                (((1,), (1,)), ((), ())),
                preferred_element_type=jnp.float32,
            )
            * inverse_root
        )
        usable = block_flags[None, :] > 0.5
        highest = jnp.max(jnp.where(usable, scores, -1e30), axis=1, keepdims=True)
        weights = jnp.exp(jnp.where(usable, scores - highest, -jnp.inf))
        denominator = jnp.maximum(jnp.sum(weights, axis=1, keepdims=True), 1.0)
        summed = jnp.dot(
            weights.astype(jnp.bfloat16), block_values, preferred_element_type=jnp.float32
        )
        return (summed / denominator).astype(jnp.bfloat16)

    attended = lax.map(attend, (query_rows, key_block, value_block, key_flags))
    returned = lax.all_to_all(attended, "seq", split_axis=1, concat_axis=1, tiled=True)
    home_index = gather_rows(query_slot, query_labels) * most_query + query_ranks
    outputs = gather_rows(returned, home_index)
    joined = outputs.transpose(1, 0, 2).reshape(tok_rows, -1)
    partial_out = jnp.dot(joined, out_weight, preferred_element_type=jnp.float32)
    return lax.psum_scatter(partial_out, "head", scatter_dimension=1, tiled=True).astype(
        jnp.bfloat16
    )


def solution(mesh):
    placed = (
        P("seq", None),
        P(None, None, "head"),
        P(),
        P(),
        P("head", None),
        P("head", "seq", None),
        P("head", "seq", None),
        P("head", None),
        P("head", None),
        P("head", None, None),
    )
    return jax.shard_map(
        body, mesh=mesh, in_specs=placed, out_specs=P("seq", "head"), check_vma=False
    )
```

profile of v0, /device:TPU:0, one launch (start us, length us, event | category | flops | bytes accessed | tf_op | source)
XLA Modules:
  0.0 285.6 jit_solution(7708221302788294027)
XLA Ops:
  9.7 10.3 %copy.79 = bf16[3072,3,384]{0,2,1:T(8,128)(2,1)} copy(bf16[3072,3,384]{2,0,1:T(8,128)(2,1)} %param.13) | data formatting | bytes 14155776 | tf_op args[1]
  19.9 5.6 %fusion.21 = f32[3,3,256,128]{2,3,1,0:T(8,128)S(1)} fusion(bf16[3,3,128,3072]{3,2,1,0:T(8,128)(2,1)} %bitcast.87, bf16[256,3072]{1,0:T(8,128)(2,1)} %param.12), kind=kOutput, calls=%fused_computation.38 | convolution fusion | flops 1811939328 | bytes 9830400 | tf_op jit(solution)/shard_map/dot_general | solution.py:64
  29.6 9.3 %gather_fusion.4 = bf16[960,128]{1,0:T(8,128)(2,1)S(1)} fusion(bf16[3,256,128]{2,1,0:T(8,128)(2,1)S(1)} %copy.80, s32[960]{0:T(1024)S(1)} %reshape.251), kind=kCustom, calls=%fused_computation.4 | custom fusion | bytes 499200 | tf_op jit(solution)/shard_map/vmap()/gather | solution.py:20
  38.9 2.3 copy_select_fusion.2
  41.1 7.3 %all-to-all-start.1 = ((bf16[3,320,128]{2,0,1:T(4,128)(2,1)}), bf16[3,320,128]{2,0,1:T(4,128)(2,1)}, u32[]{:S(2)}, u32[]{:S(2)}) async-start(bf16[3,320,128]{2,0,1:T(4,128)(2,1)} %copy_select_fusion.2), calls=%async_computation.1 | async-start | bytes 655360 | tf_op jit(solution)/shard_map/all_to_all | solution.py:83
  48.4 1.0 fusion.25
  49.5 1.7 fusion.18
  51.2 1.7 and_reduce_fusion
  54.2 1.7 gather_fusion
  56.0 2.2 gather_fusion.5
  58.5 30.3 %gather_fusion.6 = bf16[3072,128]{1,0:T(8,128)(2,1)} fusion(bf16[3,256,128]{2,1,0:T(8,128)(2,1)S(1)} %copy.83, s32[3072]{0:T(1024)S(1)} %reshape.263), kind=kCustom, calls=%fused_computation.6 | custom fusion | bytes 1597440 | tf_op jit(solution)/shard_map/vmap()/gather | solution.py:20
  88.8 30.2 %gather_fusion.7 = bf16[3072,128]{1,0:T(8,128)(2,1)} fusion(bf16[3,256,128]{2,1,0:T(8,128)(2,1)S(1)} %copy.85, s32[3072]{0:T(1024)S(1)} %reshape.263), kind=kCustom, calls=%fused_computation.7 | custom fusion | bytes 1597440 | tf_op jit(solution)/shard_map/vmap()/gather | solution.py:20
  119.0 2.4 gather_fusion.1
  122.1 10.0 %copy_select_fusion = (bf16[3,1024,128]{2,0,1:T(4,128)(2,1)}, bf16[3,1024,128]{2,0,1:T(4,128)(2,1)S(1)}) fusion(bf16[3,1024,128]{2,1,0:T(8,128)(2,1)} %bitcast.89, pred[3,1024]{0,1:T(8,128)(4,1)S(1)} %copy.82, bf16[3,1024,128]{2,1,0:T(8,128)(2,1)} %bitcast.88), kind=kLoop, calls=%fused_computation.41 | loop fusion | flops 786432 | bytes 3148800 | tf_op jit(solution)/shard_map/jit(_where)/select_n | solution.py:25
  132.0 31.1 %all_to_all.29 = bf16[3,1024,128]{2,0,1:T(4,128)(2,1)} all-to-all(bf16[3,1024,128]{2,0,1:T(4,128)(2,1)S(1)} %get-tuple-element.81), channel_id=1, replica_groups=mesh['seq'=8,'head'=4] {'seq'}, dimensions={1} | all-to-all | bytes 1572864 | tf_op jit(solution)/shard_map/all_to_all | solution.py:90
  163.2 3.7 %all-to-all-start.3 = ((bf16[3,1024,128]{2,0,1:T(4,128)(2,1)}), bf16[3,1024,128]{2,0,1:T(4,128)(2,1)S(1)}, u32[]{:S(2)}, u32[]{:S(2)}) async-start(bf16[3,1024,128]{2,0,1:T(4,128)(2,1)} %get-tuple-element.80), calls=%async_computation.3 | async-start | bytes 2097152 | tf_op jit(solution)/shard_map/all_to_all | solution.py:91
  167.6 24.7 %all-to-all-done.3 = bf16[3,1024,128]{2,0,1:T(4,128)(2,1)S(1)} async-done(((bf16[3,1024,128]{2,0,1:T(4,128)(2,1)}), bf16[3,1024,128]{2,0,1:T(4,128)(2,1)S(1)}, u32[]{:S(2)}, u32[]{:S(2)}) %all-to-all-start.3) | async-done | bytes 786464 | tf_op jit(solution)/shard_map/all_to_all | solution.py:91
  192.4 3.6 %all-to-all-start = ((bf16[3,8,128]{2,0,1:T(4,128)(2,1)}), bf16[3,8,128]{2,0,1:T(4,128)(2,1)S(1)}, u32[]{:S(2)}, u32[]{:S(2)}) async-start(bf16[3,8,128]{2,0,1:T(4,128)(2,1)} %copy.75), calls=%async_computation | async-start | bytes 16384 | tf_op jit(solution)/shard_map/all_to_all | solution.py:92
  196.0 6.6 %gather_fusion.8 = s32[768]{0:T(1024)S(1)} fusion(s32[3,8]{1,0:T(4,128)S(1)} %copy-done.1, s32[768]{0:T(1024)S(1)} %reshape.275), kind=kCustom, calls=%fused_computation.8 | custom fusion | bytes 12288 | tf_op jit(solution)/shard_map/vmap()/gather | solution.py:20
  202.6 1.1 copy.88
  203.7 1.3 copy.89
  206.0 8.7 %while.10 = (s32[]{:T(128)}, bf16[3,320,128]{2,1,0:T(8,128)(2,1)}, bf16[3,1024]{1,0:T(4,128)(2,1)S(1)}, bf16[3,320,128]{2,1,0:T(8,128)(2,1)S(1)}, bf16[3,1024,12...) while((s32[]{:T(128)}, bf16[3,320,128]{2,1,0:T(8,128)(2,1)}, ...), condition=%wide.region_13.14_spmd, body=%wide.region_10.13_spmd.sunk | while | flops 170805952 | bytes 4637521 | solution.py:116
  206.9 2.0 fusion.57
  209.8 2.0 fusion.57
  212.7 2.0 fusion.57
  214.7 1.9 copy.91
  216.6 5.8 %all-to-all-start.4 = ((bf16[3,320,128]{2,0,1:T(4,128)(2,1)}), bf16[3,320,128]{2,0,1:T(4,128)(2,1)S(1)}, u32[]{:S(2)}, u32[]{:S(2)}) async-start(bf16[3,320,128]{2,0,1:T(4,128)(2,1)} %copy.91), calls=%async_computation.4 | async-start | bytes 655360 | tf_op jit(solution)/shard_map/all_to_all | solution.py:117
  222.5 9.8 %all-to-all-done.4 = bf16[3,320,128]{2,0,1:T(4,128)(2,1)S(1)} async-done(((bf16[3,320,128]{2,0,1:T(4,128)(2,1)}), bf16[3,320,128]{2,0,1:T(4,128)(2,1)S(1)}, u32[]{:S(2)}, u32[]{:S(2)}) %all-to-all-start.4) | async-done | bytes 245792 | tf_op jit(solution)/shard_map/all_to_all | solution.py:117
  232.3 4.4 %gather_fusion.9 = bf16[768,128]{1,0:T(8,128)(2,1)S(1)} fusion(bf16[3,320,128]{2,1,0:T(8,128)(2,1)S(1)} %copy.95, s32[768]{0:T(1024)S(1)} %reshape.281), kind=kCustom, calls=%fused_computation.9 | custom fusion | bytes 399360 | tf_op jit(solution)/shard_map/vmap()/gather | solution.py:20
  236.9 2.7 fusion.46
  239.6 37.2 %reduce-scatter.2.cloned.1.call-done = f32[256,768]{1,0:T(8,128)} async-done(((f32[256,3072]{1,0:T(8,128)}), f32[256,768]{1,0:T(8,128)}) %reduce-scatter.2.cloned.1.call-update) | async-done | bytes 786448 | tf_op jit(solution)/shard_map/reduce_scatter | solution.py:122
  276.8 1.9 convert_element_type.39
  (94 shorter events, 14.1 us)
Async XLA Ops:
  6.5 230.4 %copy-start = (bf16[384,3072]{1,0:T(8,128)(2,1)S(1)}, bf16[384,3072]{1,0:T(8,128)(2,1)}, u32[]{:S(2)}) copy-start(bf16[384,3072]{1,0:T(8,128)(2,1)} %param.16) | copy-start | bytes 7077892
  19.9 5.7 %copy-start.9 = (f32[128]{0:T(128)S(1)}, f32[128]{0:T(128)}, u32[]{:S(2)}) copy-start(f32[128]{0:T(128)} %param.15) | copy-start | bytes 1540
  19.9 5.7 %copy-start.10 = (f32[128]{0:T(128)S(1)}, f32[128]{0:T(128)}, u32[]{:S(2)}) copy-start(f32[128]{0:T(128)} %param.14) | copy-start | bytes 1540
  25.5 1.0 copy-start.4
  25.5 1.2 copy-start.1
  38.9 14.2 %copy-start.8 = (s32[3,32]{1,0:T(4,128)S(1)}, s32[3,32]{1,0:T(4,128)}, u32[]{:S(2)}) copy-start(s32[3,32]{1,0:T(4,128)} %param.20) | copy-start | bytes 1156
  38.9 14.3 %copy-start.7 = (s32[3,8,8]{2,1,0:T(8,128)S(1)}, s32[3,8,8]{2,1,0:T(8,128)}, u32[]{:S(2)}) copy-start(s32[3,8,8]{2,1,0:T(8,128)} %param.21) | copy-start | bytes 2308
  41.1 90.9 %all-to-all-start.1 = ((bf16[3,320,128]{2,0,1:T(4,128)(2,1)}), bf16[3,320,128]{2,0,1:T(4,128)(2,1)}, u32[]{:S(2)}, u32[]{:S(2)}) async-start(bf16[3,320,128]{2,0,1:T(4,128)(2,1)} %copy_select_fusion.2), calls=%async_computation.1 | async-start | bytes 655360 | tf_op jit(solution)/shard_map/all_to_all | solution.py:83
  121.5 0.6 copy-start.5
  163.2 3.7 %copy-start.6 = (pred[192,16]{1,0:T(8,128)(4,1)S(1)}, pred[192,16]{1,0:T(8,128)(4,1)}, u32[]{:S(2)}) copy-start(pred[192,16]{1,0:T(8,128)(4,1)} %copy-done.5) | copy-start | bytes 9220
  163.2 29.2 %all-to-all-start.3 = ((bf16[3,1024,128]{2,0,1:T(4,128)(2,1)}), bf16[3,1024,128]{2,0,1:T(4,128)(2,1)S(1)}, u32[]{:S(2)}, u32[]{:S(2)}) async-start(bf16[3,1024,128]{2,0,1:T(4,128)(2,1)} %get-tuple-element.80), calls=%async_computation.3 | async-start | bytes 2097152 | tf_op jit(solution)/shard_map/all_to_all | solution.py:91
  192.4 3.6 %copy-start.2 = (bf16[3,1024,128]{2,0,1:T(4,128)(2,1)}, bf16[3,1024,128]{2,0,1:T(4,128)(2,1)S(1)}, u32[]{:S(2)}) copy-start(bf16[3,1024,128]{2,0,1:T(4,128)(2,1)S(1)} %all-to-all-done.3) | copy-start | bytes 2359300
  192.4 13.7 %all-to-all-start = ((bf16[3,8,128]{2,0,1:T(4,128)(2,1)}), bf16[3,8,128]{2,0,1:T(4,128)(2,1)S(1)}, u32[]{:S(2)}, u32[]{:S(2)}) async-start(bf16[3,8,128]{2,0,1:T(4,128)(2,1)} %copy.75), calls=%async_computation | async-start | bytes 16384 | tf_op jit(solution)/shard_map/all_to_all | solution.py:92
  202.6 2.5 copy-start.3
  216.6 15.7 %all-to-all-start.4 = ((bf16[3,320,128]{2,0,1:T(4,128)(2,1)}), bf16[3,320,128]{2,0,1:T(4,128)(2,1)S(1)}, u32[]{:S(2)}, u32[]{:S(2)}) async-start(bf16[3,320,128]{2,0,1:T(4,128)(2,1)} %copy.91), calls=%async_computation.4 | async-start | bytes 655360 | tf_op jit(solution)/shard_map/all_to_all | solution.py:117
  222.4 54.4 %reduce-scatter.2.cloned.1.call-start = ((), (), s32[]{:S(2)}) async-start(), calls=%async_computation.6 | async-start | bytes 3932160 | tf_op jit(solution)/shard_map/reduce_scatter | solution.py:122
Sparse Core Ops, SparseCore 0:
  239.7 37.0 reduce-scatter.1
where the time goes:
time: 287 us; the launch traced here: 286 us
  local copies, waits for them, and re-layouts  110 us (38%)
  waiting for transfers between devices  71.8 us (25%)
  blocking collectives  31.1 us (11%)
  other arithmetic  23.1 us (8%)
  starting transfers between devices  20.3 us (7%)
  matrix products  15.5 us (5%)
  between operations  13.8 us (5%)
    gather x20, local copies, waits for them, and re-layouts, gather_rows(): return jax.vmap(lambda single, lookup: single[lookup])(table, indices)  89.3 us
    reduce_scatter x1, waiting for transfers between devices, body(): lax.psum_scatter(partial_out, 'head', scatter_dimension=1, tiled=True)  37.2 us
    all_to_all x1, blocking collectives, body(): lax.all_to_all(direct_keys, 'seq', split_axis=1, concat_axis=1, tiled=True)  31.1 us
    all_to_all x1, waiting for transfers between devices, body(): lax.all_to_all(direct_values, 'seq', split_axis=1, concat_axis=1, tiled=T...  24.7 us
    select_n x2, other arithmetic, take_rows(): return jnp.where(present[..., None], picked, jnp.zeros((), picked.dtype))  12.2 us
    unnamed x26, local copies, waits for them, and re-layouts  12.1 us
    all_to_all x1, waiting for transfers between devices, body(): lax.all_to_all(attended, 'seq', split_axis=1, concat_axis=1, tiled=True)  9.8 us
    all_to_all x1, starting transfers between devices, body(): lax.all_to_all(query_send, 'seq', split_axis=1, concat_axis=1, tiled=True)  7.26 us
  transfers between devices with their start and end apart: 5, of which 3 were waited for; matrix products, arithmetic and copies ran while one was open for 33% of the time, Pallas kernels for 0%

commit v1 on v0

v1 whole, which is shorter than its diff:
```python
import functools
import math

import jax
import jax.numpy as jnp
from jax import lax
from jax.experimental import pallas as pl
from jax.experimental.pallas import tpu as pltpu
from jax.sharding import PartitionSpec as P

EPSILON = 1e-06
NEG = -2e30
START = -1e30
MESH = pl.DeviceIdType.MESH
LANES = 128
INFO = 16


def normalize(projected, gain):
    mean_square = jnp.mean(projected * projected, axis=-1, keepdims=True)
    return projected * lax.rsqrt(mean_square + EPSILON) * gain


def ring_index(position, n):
    return jnp.where(position < n // 2, 2 * position, 2 * (n - 1 - position) + 1)


def kernel(
    n, groups, tok_ref, wqkv_ref, qg_ref, kg_ref, wout_ref, neg_ref, info_ref, out_ref,
    tok_v, w_v, kv, q_v, m_s, l_s, acc_s, att, wall,
    load_sem, right_send, right_recv, left_send, left_recv,
    att_send, att_recv, wt_send, wt_recv,
):
    heads, rows, width = q_v.shape
    cols = out_ref.shape[1]
    half = n // 2
    seq = lax.axis_index("seq")
    mine = lax.axis_index("head")
    pos = jnp.where(seq % 2 == 0, seq // 2, n - 1 - seq // 2)
    right = ring_index((pos + 1) % n, n)
    left = ring_index((pos + n - 1) % n, n)

    tok_load = pltpu.make_async_copy(tok_ref, tok_v, load_sem.at[0])
    tok_load.start()
    w_loads = [pltpu.make_async_copy(wqkv_ref.at[j], w_v.at[j], load_sem.at[1 + j]) for j in range(3)]
    for j in (1, 2, 0):
        w_loads[j].start()
    own_cols = pl.ds(pl.multiple_of(mine * cols, LANES), cols)
    own_load = pltpu.make_async_copy(wout_ref.at[:, :, own_cols], wall.at[:, mine], load_sem.at[4])
    own_load.start()

    barrier = pltpu.get_barrier_semaphore()
    for neighbour in (left, right):
        pl.semaphore_signal(barrier, inc=1, device_id={"seq": neighbour}, device_id_type=MESH)
    for offset in range(1, groups):
        pl.semaphore_signal(
            barrier, inc=1, device_id={"head": (mine + offset) % groups}, device_id_type=MESH
        )

    def rightward(slot, h, hop, low, size):
        part = kv.at[slot, h, pl.ds(low, size)]
        return pltpu.make_async_remote_copy(
            src_ref=part, dst_ref=part, send_sem=right_send.at[hop, h],
            recv_sem=right_recv.at[hop, h], device_id={"seq": right}, device_id_type=MESH,
        )

    def leftward(slot, h, hop, low, size):
        part = kv.at[slot, h, pl.ds(low, size)]
        return pltpu.make_async_remote_copy(
            src_ref=part, dst_ref=part, send_sem=left_send.at[hop, h],
            recv_sem=left_recv.at[hop, h], device_id={"seq": left}, device_id_type=MESH,
        )

    full = (0, 2 * rows + INFO)
    key_part = (rows, rows + INFO)
    value_part = (0, rows)

    def weights_copy(offset):
        peer = (mine + offset) % groups
        peer_cols = pl.ds(pl.multiple_of(peer * cols, LANES), cols)
        return pltpu.make_async_remote_copy(
            src_ref=wout_ref.at[:, :, peer_cols], dst_ref=wall.at[:, mine],
            send_sem=wt_send.at[offset], recv_sem=wt_recv.at[offset],
            device_id={"head": peer}, device_id_type=MESH,
        )

    def att_copy(offset, h):
        peer = (mine + offset) % groups
        return pltpu.make_async_remote_copy(
            src_ref=att.at[h, mine], dst_ref=att.at[h, mine],
            send_sem=att_send.at[offset, h], recv_sem=att_recv.at[offset, h],
            device_id={"head": peer}, device_id_type=MESH,
        )

    tok_load.wait()
    w_loads[1].wait()
    keys = jnp.dot(tok_v[...], w_v[1], preferred_element_type=jnp.float32)
    for h in range(heads):
        kv[pos, h, pl.ds(rows, rows)] = normalize(
            keys[:, h * width : (h + 1) * width], kg_ref[...]
        ).astype(jnp.bfloat16)
        kv[pos, h, pl.ds(2 * rows, INFO)] = info_ref[h]
    w_loads[2].wait()
    values = jnp.dot(tok_v[...], w_v[2], preferred_element_type=jnp.float32)
    for h in range(heads):
        kv[pos, h, pl.ds(0, rows)] = values[:, h * width : (h + 1) * width].astype(jnp.bfloat16)

    pl.semaphore_wait(barrier, 1 + groups)
    for h in range(heads):
        rightward(pos, h, 0, *full).start()
        leftward(pos, h, 0, *full).start()
    for offset in range(1, groups):
        weights_copy(offset).start()

    w_loads[0].wait()
    queries = jnp.dot(tok_v[...], w_v[0], preferred_element_type=jnp.float32)
    for h in range(heads):
        q_v[h] = normalize(queries[:, h * width : (h + 1) * width], qg_ref[...]).astype(
            jnp.bfloat16
        )
    m_s[...] = jnp.full(m_s.shape, START, jnp.float32)
    l_s[...] = jnp.zeros(l_s.shape, jnp.float32)
    acc_s[...] = jnp.zeros(acc_s.shape, jnp.float32)
    factor = math.log2(math.e) / math.sqrt(width)

    def attend(slot, h):
        block_values = kv[slot, h, pl.ds(0, rows)]
        block_keys = kv[slot, h, pl.ds(rows, rows)]
        info = kv[slot, h, pl.ds(2 * rows, INFO)].astype(jnp.float32)
        row = jnp.concatenate([info[r : r + 1, :] for r in range(rows // LANES)], axis=1)
        slots = neg_ref.shape[2]
        ids = lax.broadcasted_iota(jnp.int32, (slots, rows), 0).astype(jnp.float32)
        owner = jnp.where(ids == row, 1.0, 0.0).astype(jnp.bfloat16)
        scores = lax.dot_general(
            q_v[h], block_keys, (((1,), (1,)), ((), ())), preferred_element_type=jnp.float32
        ) + jnp.dot(neg_ref[h], owner, preferred_element_type=jnp.float32)
        before = m_s[h][:, :1]
        highest = jnp.maximum(before, jnp.max(scores, axis=1, keepdims=True))
        weights = jnp.exp2((scores - highest) * factor)
        shrink = jnp.exp2((before - highest) * factor)
        total = l_s[h][:, :1] * shrink + jnp.sum(weights, axis=1, keepdims=True)
        summed = acc_s[h] * shrink + jnp.dot(
            weights.astype(jnp.bfloat16), block_values, preferred_element_type=jnp.float32
        )
        m_s[h] = jnp.broadcast_to(highest, (rows, width))
        l_s[h] = jnp.broadcast_to(total, (rows, width))
        acc_s[h] = summed

    def each_head(action):
        lax.fori_loop(0, heads, lambda h, c: (action(h), c)[1], 0)

    each_head(lambda h: attend(pos, h))

    def passing(hop, right_next, left_next):
        from_left = (pos + n - hop) % n
        from_right = (pos + hop) % n

        def forward(h):
            rightward(from_left, h, hop - 1, *full).wait_recv()
            rightward(from_left, h, hop, *right_next).start()
            leftward(from_right, h, hop - 1, *full).wait_recv()
            leftward(from_right, h, hop, *left_next).start()

        def work(h):
            attend(from_left, h)
            attend(from_right, h)

        each_head(forward)
        each_head(work)

    lax.fori_loop(1, half - 1, lambda hop, c: (passing(hop, full, full), c)[1], 0)
    passing(half - 1, key_part, value_part)

    opposite = (pos + half) % n
    for h in range(heads):
        rightward(opposite, h, half - 1, *key_part).wait_recv()
        leftward(opposite, h, half - 1, *value_part).wait_recv()
        attend(opposite, h)
        att[h, mine] = (acc_s[h] / jnp.maximum(l_s[h], 1.0)).astype(jnp.bfloat16)
        for offset in range(1, groups):
            att_copy(offset, h).start()

    own_load.wait()
    for offset in range(1, groups):
        weights_copy(offset).wait_recv()
    result = None
    for h in range(heads):
        for offset in range(1, groups):
            att_copy(offset, h).wait_recv()
        joined = jnp.concatenate([att[h, g] for g in range(groups)], axis=1)
        part = jnp.dot(
            joined, wall[h].reshape(groups * width, cols), preferred_element_type=jnp.float32
        )
        result = part if result is None else result + part
    out_ref[...] = result.astype(out_ref.dtype)

    for offset in range(1, groups):
        weights_copy(offset).wait_send()
        for h in range(heads):
            att_copy(offset, h).wait_send()

    def drain(hop):
        def one(h):
            rightward(pos, h, hop, *full).wait_send()
            leftward(pos, h, hop, *full).wait_send()

        each_head(one)

    lax.fori_loop(0, half - 1, lambda hop, c: (drain(hop), c)[1], 0)
    for h in range(heads):
        rightward(pos, h, half - 1, *key_part).wait_send()
        leftward(pos, h, half - 1, *value_part).wait_send()


def body(
    tokens, qkv_weight, q_gain, k_gain, out_weight,
    query_cluster, key_cluster, query_slot, key_slot, pairs,
):
    n = lax.axis_size("seq")
    groups = lax.axis_size("head")
    rows, depth = tokens.shape
    heads = pairs.shape[0]
    width = q_gain.shape[0]
    key_clusters = key_slot.shape[1]
    members = query_slot.shape[1]
    slots = -(-key_clusters // LANES) * LANES
    cols = out_weight.shape[1] // groups

    ids = jnp.arange(slots, dtype=jnp.int32)
    listed = jnp.any(pairs[:, :, :, None] == ids, axis=2)
    member_ids = jnp.arange(members, dtype=jnp.int32)
    placed = query_slot[:, :, None] == member_ids
    named = query_cluster == member_ids
    owner = jnp.einsum(
        "htc,hcr->htr", named.astype(jnp.bfloat16), placed.astype(jnp.bfloat16),
        preferred_element_type=jnp.float32,
    ).astype(jnp.bfloat16)
    allowed = jnp.einsum(
        "htr,hrs->hts", owner, listed.astype(jnp.bfloat16), preferred_element_type=jnp.float32
    )
    neg = jnp.where(allowed > 0.5, 0.0, NEG).astype(jnp.bfloat16)
    cluster_ids = jnp.arange(key_clusters, dtype=jnp.int32)
    located = jnp.sum(
        jnp.where(key_cluster == cluster_ids, key_slot[:, None, :], 0), axis=2
    ).astype(jnp.bfloat16)
    info = located.reshape(heads, rows // LANES, LANES)
    info = jnp.pad(info, ((0, 0), (0, INFO - rows // LANES), (0, 0)))

    vmem = pl.BlockSpec(memory_space=pltpu.VMEM)
    anywhere = pl.BlockSpec(memory_space=pl.ANY)
    dma = pltpu.SemaphoreType.DMA
    bf16 = jnp.bfloat16
    return pl.pallas_call(
        functools.partial(kernel, n, groups),
        out_shape=jax.ShapeDtypeStruct((rows, cols), bf16),
        in_specs=[anywhere, anywhere, vmem, vmem, anywhere, vmem, vmem],
        out_specs=vmem,
        scratch_shapes=[
            pltpu.VMEM((rows, depth), bf16),
            pltpu.VMEM((3, depth, heads * width), bf16),
            pltpu.VMEM((n, heads, 2 * rows + INFO, width), bf16),
            pltpu.VMEM((heads, rows, width), bf16),
            pltpu.VMEM((heads, rows, width), jnp.float32),
            pltpu.VMEM((heads, rows, width), jnp.float32),
            pltpu.VMEM((heads, rows, width), jnp.float32),
            pltpu.VMEM((heads, groups, rows, width), bf16),
            pltpu.VMEM((heads, groups, width, cols), bf16),
            dma((5,)),
            dma((n // 2, heads)),
            dma((n // 2, heads)),
            dma((n // 2, heads)),
            dma((n // 2, heads)),
            dma((groups, heads)),
            dma((groups, heads)),
            dma((groups,)),
            dma((groups,)),
        ],
        compiler_params=pltpu.CompilerParams(
            collective_id=0, has_side_effects=True, vmem_limit_bytes=56 * 1024 * 1024
        ),
        cost_estimate=pl.CostEstimate(
            flops=2 * rows * depth * 4 * heads * width, bytes_accessed=12 * 1024 * 1024,
            transcendentals=heads * rows * rows * n,
        ),
    )(
        tokens,
        qkv_weight.transpose(1, 0, 2),
        q_gain.reshape(1, width),
        k_gain.reshape(1, width),
        out_weight.reshape(heads, width, out_weight.shape[1]),
        neg,
        info,
    )


def solution(mesh):
    placed = (
        P("seq", None),
        P(None, None, "head"),
        P(),
        P(),
        P("head", None),
        P("head", "seq", None),
        P("head", "seq", None),
        P("head", None),
        P("head", None),
        P("head", None, None),
    )
    return jax.shard_map(
        body, mesh=mesh, in_specs=placed, out_specs=P("seq", "head"), check_vma=False
    )
```

time: 287 us -> 57.6 us (0.20)
  local copies, waits for them, and re-layouts: 110 us -> 3.76 us
  waiting for transfers between devices: 71.8 us -> 0 us
  Pallas kernels: 0 us -> 49.9 us
  blocking collectives: 31.1 us -> 0 us
  other arithmetic: 23.1 us -> 1.59 us
  starting transfers between devices: 20.3 us -> 0 us
  between operations: 13.8 us -> 0.03 us
  matrix products: 15.5 us -> 1.92 us
    gather x20 -> x0, local copies, waits for them, and re-layouts: 89.3 us -> none  [gather_rows(): return jax.vmap(lambda single, lookup: single[lookup])(table, indices)]
    pallas_call x0 -> x1, Pallas kernels: none -> 49.9 us  [body(): pl.pallas_call(functools.partial(kernel, n, groups), out_shape=jax.ShapeD...]
    reduce_scatter x1 -> x0, waiting for transfers between devices: 37.2 us -> none  [body(): lax.psum_scatter(partial_out, 'head', scatter_dimension=1, tiled=True)]
    all_to_all x4 -> x0, waiting for transfers between devices: 34.5 us -> none  [the longest x1 24.7 us: body(): lax.all_to_all(direct_values, 'seq', split_axis=1, concat_axis=1, tiled=T...]
    all_to_all x1 -> x0, blocking collectives: 31.1 us -> none  [body(): lax.all_to_all(direct_keys, 'seq', split_axis=1, concat_axis=1, tiled=True)]
    all_to_all x4 -> x0, starting transfers between devices: 20.3 us -> none  [the longest x1 7.26 us: body(): lax.all_to_all(query_send, 'seq', split_axis=1, concat_axis=1, tiled=True)]
    dot_general x8 -> x1, matrix products: 15.5 us -> 1.92 us  [body(): jnp.einsum('htr,hrs->hts', owner, listed.astype(jnp.bfloat16), preferred_...]
    select_n x2 -> x0, other arithmetic: 12.2 us -> none  [take_rows(): return jnp.where(present[..., None], picked, jnp.zeros((), picked.dtype))]
  transfers between devices with their start and end apart: 5 -> 0, of which waited for: 3 -> 0; matrix products, arithmetic and copies ran while one was open for 33% -> 0% of each run, Pallas kernels for 0% -> 0%
where the time goes in v1:
time: 57.6 us; the launch traced here: 57.2 us
  Pallas kernels  49.9 us (87%)
  local copies, waits for them, and re-layouts  3.76 us (7%)
  matrix products  1.92 us (3%)
  other arithmetic  1.59 us (3%)
    pallas_call x1, Pallas kernels, body(): pl.pallas_call(functools.partial(kernel, n, groups), out_shape=jax.ShapeD...  49.9 us
    unnamed x3, local copies, waits for them, and re-layouts  3.14 us
    dot_general x1, matrix products, body(): jnp.einsum('htr,hrs->hts', owner, listed.astype(jnp.bfloat16), preferred_...  1.92 us

profile of v1, /device:TPU:0, one launch (start us, length us, event | category | flops | bytes accessed | tf_op | source)
XLA Modules:
  0.0 57.2 jit_solution(14903924132046189474)
XLA Ops:
  0.0 0.8 %fusion.4 = pred[3,8,128]{2,1,0:T(8,128)(4,1)S(1)} fusion(s32[3,8,8]{2,1,0:T(8,128)} %param.19), kind=kLoop, calls=%fused_computation.9 | loop fusion | flops 46080 | bytes 3840 | tf_op jit(solution)/shard_map/reduce_or | solution.py:230
  0.8 0.7 %copy.16 = s32[3,256,1]{1,0,2:T(4,128)S(1)} copy(s32[3,256,1]{1,2,0:T(1,128)} %param.15) | data formatting | bytes 6144
  1.5 0.7 %copy.15 = s32[3,256,1]{1,0,2:T(4,128)S(1)} copy(s32[3,256,1]{1,2,0:T(1,128)} %param.16) | data formatting | bytes 6144
  2.2 0.8 %select_reduce_fusion = s32[3,256]{1,0:T(4,128)S(1)} fusion(s32[3,32]{1,0:T(4,128)} %param.18, s32[3,256]{1,0:T(4,128)S(1)} %bitcast.13), kind=kLoop, calls=%fused_computation.6 | loop fusion | flops 72960 | bytes 6528 | tf_op jit(solution)/shard_map/reduce_sum | solution.py:243
  3.0 0.6 %pad.4.info_ref = bf16[3,16,128]{2,1,0:T(8,128)(2,1)} pad(bf16[3,2,128]{2,1,0:T(2,128)(2,1)S(1)} %convert_element_type.21, bf16[]{:T(256)} %constant.11.clone.1), padding=0_0x0_14x0_0 | pad | bytes 13826 | tf_op jit(solution)/shard_map/jit(_pad)/pad | solution.py:247
  3.6 1.9 %fusion.1.neg_ref = bf16[3,256,128]{2,1,0:T(8,128)(2,1)} fusion(pred[3,8,128]{2,1,0:T(8,128)(4,1)S(1)} %fusion.4, s32[3,256]{1,0:T(4,128)S(1)} %bitcast.14, s32[3,8]{1,0:T(4,128)} %param.17), kind=kOutput, calls=%fused_computation.2 | convolution fusion | flops 1978560 | bytes 202848 | tf_op jit(solution)/shard_map/htr,hrs->hts/dot_general | solution.py:238
  5.5 49.9 %shard_map.100 = bf16[256,768]{1,0:T(8,128)(2,1)} custom-call(bf16[256,3072]{1,0:T(8,128)(2,1)} %tok_ref.1, bf16[3,3072,384]{2,1,0:T(8,128)(2,1)} %bitcast.11, f32[1,128]{1,0:T(1,128)} %bitcast.15, f32[1,128]{1,0:T(1,128)} %bitcast.16, bf16[3,128,3072]{2,1,0:T(8,128)(2,1)} %bitcast.12, bf16[3,256,128]{2,1,0:T(8,128)(2,1)} %fusion.1.neg_ref, ...), custom_call_target="tpu_custom_call" | custom-call | flops 2415919104 | bytes 12582912 | tf_op jit(solution)/shard_map/pallas_call | solution.py:253
  55.5 1.8 %copy.18 = bf16[256,768]{1,0:T(8,128)(2,1)} copy(bf16[256,768]{1,0:T(8,128)(2,1)} %shard_map.100) | data formatting | bytes 786432
  (2 shorter events, 0.0 us)

commit v2 on v1

--- a/solution.py
+++ b/solution.py
@@ -25,9 +25,16 @@
     return jnp.where(position < n // 2, 2 * position, 2 * (n - 1 - position) + 1)
 
 
+def look_up(labels, table_ref, h):
+    found = jnp.zeros(labels.shape, jnp.int32)
+    for c in range(table_ref.shape[1]):
+        found = jnp.where(labels == c, table_ref[h, c], found)
+    return found
+
+
 def kernel(
-    n, groups, tok_ref, wqkv_ref, qg_ref, kg_ref, wout_ref, neg_ref, info_ref, out_ref,
-    tok_v, w_v, kv, q_v, m_s, l_s, acc_s, att, wall,
+    n, groups, tok_ref, wqkv_ref, qg_ref, kg_ref, wout_ref, qc_ref, kc_ref, qslot_ref, kslot_ref,
+    pairs_ref, out_ref, tok_v, w_v, kv, q_v, neg_s, m_s, l_s, acc_s, att, wall,
     load_sem, right_send, right_recv, left_send, left_recv,
     att_send, att_recv, wt_send, wt_recv,
 ):
@@ -84,13 +91,22 @@
             device_id={"head": peer}, device_id_type=MESH,
         )
 
-    def att_copy(offset, h):
-        peer = (mine + offset) % groups
+    near = mine + 1 - 2 * (mine % 2)
+    far = (mine + 2) % groups
+
+    def att_copy(kind, h):
+        block = far if kind == 2 else mine
         return pltpu.make_async_remote_copy(
-            src_ref=att.at[h, mine], dst_ref=att.at[h, mine],
-            send_sem=att_send.at[offset, h], recv_sem=att_recv.at[offset, h],
-            device_id={"head": peer}, device_id_type=MESH,
-        )
+            src_ref=att.at[h, block], dst_ref=att.at[h, block],
+            send_sem=att_send.at[kind, h], recv_sem=att_recv.at[kind, h],
+            device_id={"head": far if kind == 1 else near}, device_id_type=MESH,
+        )
+
+    for h in range(heads):
+        placed = look_up(kc_ref[h], kslot_ref, h).astype(jnp.float32)
+        lines = [placed[:, r * LANES : (r + 1) * LANES] for r in range(rows // LANES)]
+        lines.append(jnp.zeros((INFO - rows // LANES, LANES), jnp.float32))
+        kv[pos, h, pl.ds(2 * rows, INFO)] = jnp.concatenate(lines, axis=0).astype(jnp.bfloat16)
 
     tok_load.wait()
     w_loads[1].wait()
@@ -99,7 +115,6 @@
         kv[pos, h, pl.ds(rows, rows)] = normalize(
             keys[:, h * width : (h + 1) * width], kg_ref[...]
         ).astype(jnp.bfloat16)
-        kv[pos, h, pl.ds(2 * rows, INFO)] = info_ref[h]
     w_loads[2].wait()
     values = jnp.dot(tok_v[...], w_v[2], preferred_element_type=jnp.float32)
     for h in range(heads):
@@ -118,6 +133,23 @@
         q_v[h] = normalize(queries[:, h * width : (h + 1) * width], qg_ref[...]).astype(
             jnp.bfloat16
         )
+    members, lists = pairs_ref.shape[1:]
+    slots = neg_s.shape[2]
+    padded = -(-members // LANES) * LANES
+    member_ids = lax.broadcasted_iota(jnp.int32, (padded, rows), 0)
+    slot_ids = lax.broadcasted_iota(jnp.int32, (members, slots), 1)
+    for h in range(heads):
+        owners = look_up(qc_ref[h], qslot_ref, h)
+        owned = jnp.where(member_ids == owners, 1.0, 0.0).T.astype(jnp.bfloat16)
+        entries = pairs_ref[h]
+        listed = jnp.zeros((members, slots), jnp.float32)
+        for k in range(lists):
+            listed = jnp.where(entries[:, k : k + 1] == slot_ids, 1.0, listed)
+        if padded > members:
+            blank = jnp.zeros((padded - members, slots), jnp.float32)
+            listed = jnp.concatenate([listed, blank], axis=0)
+        allowed = jnp.dot(owned, listed.astype(jnp.bfloat16), preferred_element_type=jnp.float32)
+        neg_s[h] = jnp.where(allowed > 0.5, 0.0, NEG).astype(jnp.bfloat16)
     m_s[...] = jnp.full(m_s.shape, START, jnp.float32)
     l_s[...] = jnp.zeros(l_s.shape, jnp.float32)
     acc_s[...] = jnp.zeros(acc_s.shape, jnp.float32)
@@ -128,12 +160,11 @@
         block_keys = kv[slot, h, pl.ds(rows, rows)]
         info = kv[slot, h, pl.ds(2 * rows, INFO)].astype(jnp.float32)
         row = jnp.concatenate([info[r : r + 1, :] for r in range(rows // LANES)], axis=1)
-        slots = neg_ref.shape[2]
         ids = lax.broadcasted_iota(jnp.int32, (slots, rows), 0).astype(jnp.float32)
         owner = jnp.where(ids == row, 1.0, 0.0).astype(jnp.bfloat16)
         scores = lax.dot_general(
             q_v[h], block_keys, (((1,), (1,)), ((), ())), preferred_element_type=jnp.float32
-        ) + jnp.dot(neg_ref[h], owner, preferred_element_type=jnp.float32)
+        ) + jnp.dot(neg_s[h], owner, preferred_element_type=jnp.float32)
         before = m_s[h][:, :1]
         highest = jnp.maximum(before, jnp.max(scores, axis=1, keepdims=True))
         weights = jnp.exp2((scores - highest) * factor)
@@ -177,16 +208,22 @@
         leftward(opposite, h, half - 1, *value_part).wait_recv()
         attend(opposite, h)
         att[h, mine] = (acc_s[h] / jnp.maximum(l_s[h], 1.0)).astype(jnp.bfloat16)
-        for offset in range(1, groups):
-            att_copy(offset, h).start()
+        att_copy(0, h).start()
+        att_copy(1, h).start()
+        if h > 0:
+            att_copy(1, h - 1).wait_recv()
+            att_copy(2, h - 1).start()
 
     own_load.wait()
     for offset in range(1, groups):
         weights_copy(offset).wait_recv()
     result = None
     for h in range(heads):
-        for offset in range(1, groups):
-            att_copy(offset, h).wait_recv()
+        if h == heads - 1:
+            att_copy(1, h).wait_recv()
+            att_copy(2, h).start()
+        att_copy(0, h).wait_recv()
+        att_copy(2, h).wait_recv()
         joined = jnp.concatenate([att[h, g] for g in range(groups)], axis=1)
         part = jnp.dot(
             joined, wall[h].reshape(groups * width, cols), preferred_element_type=jnp.float32
@@ -196,8 +233,9 @@
 
     for offset in range(1, groups):
         weights_copy(offset).wait_send()
-        for h in range(heads):
-            att_copy(offset, h).wait_send()
+    for h in range(heads):
+        for kind in range(3):
+            att_copy(kind, h).wait_send()
 
     def drain(hop):
         def one(h):
@@ -222,44 +260,25 @@
     heads = pairs.shape[0]
     width = q_gain.shape[0]
     key_clusters = key_slot.shape[1]
-    members = query_slot.shape[1]
     slots = -(-key_clusters // LANES) * LANES
     cols = out_weight.shape[1] // groups
 
-    ids = jnp.arange(slots, dtype=jnp.int32)
-    listed = jnp.any(pairs[:, :, :, None] == ids, axis=2)
-    member_ids = jnp.arange(members, dtype=jnp.int32)
-    placed = query_slot[:, :, None] == member_ids
-    named = query_cluster == member_ids
-    owner = jnp.einsum(
-        "htc,hcr->htr", named.astype(jnp.bfloat16), placed.astype(jnp.bfloat16),
-        preferred_element_type=jnp.float32,
-    ).astype(jnp.bfloat16)
-    allowed = jnp.einsum(
-        "htr,hrs->hts", owner, listed.astype(jnp.bfloat16), preferred_element_type=jnp.float32
-    )
-    neg = jnp.where(allowed > 0.5, 0.0, NEG).astype(jnp.bfloat16)
-    cluster_ids = jnp.arange(key_clusters, dtype=jnp.int32)
-    located = jnp.sum(
-        jnp.where(key_cluster == cluster_ids, key_slot[:, None, :], 0), axis=2
-    ).astype(jnp.bfloat16)
-    info = located.reshape(heads, rows // LANES, LANES)
-    info = jnp.pad(info, ((0, 0), (0, INFO - rows // LANES), (0, 0)))
-
     vmem = pl.BlockSpec(memory_space=pltpu.VMEM)
+    smem = pl.BlockSpec(memory_space=pltpu.SMEM)
     anywhere = pl.BlockSpec(memory_space=pl.ANY)
     dma = pltpu.SemaphoreType.DMA
     bf16 = jnp.bfloat16
     return pl.pallas_call(
         functools.partial(kernel, n, groups),
         out_shape=jax.ShapeDtypeStruct((rows, cols), bf16),
-        in_specs=[anywhere, anywhere, vmem, vmem, anywhere, vmem, vmem],
+        in_specs=[anywhere, anywhere, vmem, vmem, anywhere, vmem, vmem, smem, smem, vmem],
         out_specs=vmem,
         scratch_shapes=[
             pltpu.VMEM((rows, depth), bf16),
             pltpu.VMEM((3, depth, heads * width), bf16),
             pltpu.VMEM((n, heads, 2 * rows + INFO, width), bf16),
             pltpu.VMEM((heads, rows, width), bf16),
+            pltpu.VMEM((heads, rows, slots), bf16),
             pltpu.VMEM((heads, rows, width), jnp.float32),
             pltpu.VMEM((heads, rows, width), jnp.float32),
             pltpu.VMEM((heads, rows, width), jnp.float32),
@@ -270,8 +289,8 @@
             dma((n // 2, heads)),
             dma((n // 2, heads)),
             dma((n // 2, heads)),
-            dma((groups, heads)),
-            dma((groups, heads)),
+            dma((3, heads)),
+            dma((3, heads)),
             dma((groups,)),
             dma((groups,)),
         ],
@@ -288,8 +307,11 @@
         q_gain.reshape(1, width),
         k_gain.reshape(1, width),
         out_weight.reshape(heads, width, out_weight.shape[1]),
-        neg,
-        info,
+        query_cluster.transpose(0, 2, 1),
+        key_cluster.transpose(0, 2, 1),
+        query_slot,
+        key_slot,
+        pairs,
     )
 
 

time: 57.6 us -> 51.1 us (0.89)
  local copies, waits for them, and re-layouts: 3.76 us -> 1.77 us
  matrix products: 1.92 us -> 0 us
  other arithmetic: 1.59 us -> 0 us
  Pallas kernels: 49.9 us -> 49 us
    dot_general x1 -> x0, matrix products: 1.92 us -> none  [body(): jnp.einsum('htr,hrs->hts', owner, listed.astype(jnp.bfloat16), preferred_...]
    unnamed x3 -> x1, local copies, waits for them, and re-layouts: 3.14 us -> 1.77 us
    pallas_call x1, Pallas kernels: 49.9 us -> 49 us  [body(): pl.pallas_call(functools.partial(kernel, n, groups), out_shape=jax.ShapeD...]
    reduce_or x1 -> x0, other arithmetic: 0.81 us -> none  [body(): listed = jnp.any(pairs[:, :, :, None] == ids, axis=2)]
    reduce_sum x1 -> x0, other arithmetic: 0.77 us -> none  [body(): jnp.sum(jnp.where(key_cluster == cluster_ids, key_slot[:, None, :], 0), a...]
    pad x1 -> x0, local copies, waits for them, and re-layouts: 0.6 us -> none  [body(): info = jnp.pad(info, ((0, 0), (0, INFO - rows // LANES), (0, 0)))]
where the time goes in v2:
time: 51.1 us; the launch traced here: 50.8 us
  Pallas kernels  49 us (96%)
  local copies, waits for them, and re-layouts  1.77 us (3%)
    pallas_call x1, Pallas kernels, body(): pl.pallas_call(functools.partial(kernel, n, groups), out_shape=jax.ShapeD...  49 us
    unnamed x1, local copies, waits for them, and re-layouts  1.77 us

profile of v2, /device:TPU:0, one launch (start us, length us, event | category | flops | bytes accessed | tf_op | source)
XLA Modules:
  0.0 50.8 jit_solution(15119443169919009093)
XLA Ops:
  0.0 49.0 %shard_map.100 = bf16[256,768]{1,0:T(8,128)(2,1)} custom-call(bf16[256,3072]{1,0:T(8,128)(2,1)} %tok_ref.1, bf16[3,3072,384]{2,1,0:T(8,128)(2,1)} %bitcast.6, f32[1,128]{1,0:T(1,128)} %bitcast.10, f32[1,128]{1,0:T(1,128)} %bitcast.11, bf16[3,128,3072]{2,1,0:T(8,128)(2,1)} %bitcast.7, s32[3,1,256]{2,1,0:T(1,128)} %bitcast.8, s32[3,1,256]{2,1,0:T(1,128)} %bitcast.9, ...), custom_call_target="tpu_custom_call" | custom-call | flops 2415919104 | bytes 12582912 | tf_op jit(solution)/shard_map/pallas_call | solution.py:271
  49.0 1.8 %copy.12 = bf16[256,768]{1,0:T(8,128)(2,1)} copy(bf16[256,768]{1,0:T(8,128)(2,1)} %shard_map.100) | data formatting | bytes 786432

commit v3 on v2

--- a/solution.py
+++ b/solution.py
@@ -50,12 +50,9 @@
     tok_load = pltpu.make_async_copy(tok_ref, tok_v, load_sem.at[0])
     tok_load.start()
     w_loads = [pltpu.make_async_copy(wqkv_ref.at[j], w_v.at[j], load_sem.at[1 + j]) for j in range(3)]
-    for j in (1, 2, 0):
-        w_loads[j].start()
+    w_loads[1].start()
     own_cols = pl.ds(pl.multiple_of(mine * cols, LANES), cols)
     own_load = pltpu.make_async_copy(wout_ref.at[:, :, own_cols], wall.at[:, mine], load_sem.at[4])
-    own_load.start()
-
     barrier = pltpu.get_barrier_semaphore()
     for neighbour in (left, right):
         pl.semaphore_signal(barrier, inc=1, device_id={"seq": neighbour}, device_id_type=MESH)
@@ -110,20 +107,26 @@
 
     tok_load.wait()
     w_loads[1].wait()
+    w_loads[2].start()
+    w_loads[0].start()
     keys = jnp.dot(tok_v[...], w_v[1], preferred_element_type=jnp.float32)
     for h in range(heads):
         kv[pos, h, pl.ds(rows, rows)] = normalize(
             keys[:, h * width : (h + 1) * width], kg_ref[...]
         ).astype(jnp.bfloat16)
+    pl.semaphore_wait(barrier, 1 + groups)
+    for h in range(heads):
+        rightward(pos, h, 0, *key_part).start()
+        leftward(pos, h, 0, *key_part).start()
     w_loads[2].wait()
     values = jnp.dot(tok_v[...], w_v[2], preferred_element_type=jnp.float32)
     for h in range(heads):
         kv[pos, h, pl.ds(0, rows)] = values[:, h * width : (h + 1) * width].astype(jnp.bfloat16)
 
-    pl.semaphore_wait(barrier, 1 + groups)
-    for h in range(heads):
-        rightward(pos, h, 0, *full).start()
-        leftward(pos, h, 0, *full).start()
+    for h in range(heads):
+        rightward(pos, h, 0, *value_part).start()
+        leftward(pos, h, 0, *value_part).start()
+    own_load.start()
     for offset in range(1, groups):
         weights_copy(offset).start()
 
@@ -191,13 +194,10 @@
             rightward(from_left, h, hop, *right_next).start()
             leftward(from_right, h, hop - 1, *full).wait_recv()
             leftward(from_right, h, hop, *left_next).start()
-
-        def work(h):
             attend(from_left, h)
             attend(from_right, h)
 
         each_head(forward)
-        each_head(work)
 
     lax.fori_loop(1, half - 1, lambda hop, c: (passing(hop, full, full), c)[1], 0)
     passing(half - 1, key_part, value_part)

time: 51.1 us -> 49.2 us (0.963)
  Pallas kernels: 49 us -> 46.8 us
    pallas_call x1, Pallas kernels: 49 us -> 46.8 us  [body(): pl.pallas_call(functools.partial(kernel, n, groups), out_shape=jax.ShapeD...]
where the time goes in v3:
time: 49.2 us; the launch traced here: 48.6 us
  Pallas kernels  46.8 us (95%)
  local copies, waits for them, and re-layouts  1.77 us (4%)
    pallas_call x1, Pallas kernels, body(): pl.pallas_call(functools.partial(kernel, n, groups), out_shape=jax.ShapeD...  46.8 us
    unnamed x1, local copies, waits for them, and re-layouts  1.77 us

profile of v3, /device:TPU:0, one launch (start us, length us, event | category | flops | bytes accessed | tf_op | source)
XLA Modules:
  0.0 48.6 jit_solution(2979052513716585959)
XLA Ops:
  0.0 46.8 %shard_map.100 = bf16[256,768]{1,0:T(8,128)(2,1)} custom-call(bf16[256,3072]{1,0:T(8,128)(2,1)} %tok_ref.1, bf16[3,3072,384]{2,1,0:T(8,128)(2,1)} %bitcast.6, f32[1,128]{1,0:T(1,128)} %bitcast.10, f32[1,128]{1,0:T(1,128)} %bitcast.11, bf16[3,128,3072]{2,1,0:T(8,128)(2,1)} %bitcast.7, s32[3,1,256]{2,1,0:T(1,128)} %bitcast.8, s32[3,1,256]{2,1,0:T(1,128)} %bitcast.9, ...), custom_call_target="tpu_custom_call" | custom-call | flops 2415919104 | bytes 12582912 | tf_op jit(solution)/shard_map/pallas_call | solution.py:271
  46.8 1.8 %copy.12 = bf16[256,768]{1,0:T(8,128)(2,1)} copy(bf16[256,768]{1,0:T(8,128)(2,1)} %shard_map.100) | data formatting | bytes 786432

commit v4 on v3

--- a/solution.py
+++ b/solution.py
@@ -21,10 +21,6 @@
     return projected * lax.rsqrt(mean_square + EPSILON) * gain
 
 
-def ring_index(position, n):
-    return jnp.where(position < n // 2, 2 * position, 2 * (n - 1 - position) + 1)
-
-
 def look_up(labels, table_ref, h):
     found = jnp.zeros(labels.shape, jnp.int32)
     for c in range(table_ref.shape[1]):
@@ -35,17 +31,21 @@
 def kernel(
     n, groups, tok_ref, wqkv_ref, qg_ref, kg_ref, wout_ref, qc_ref, kc_ref, qslot_ref, kslot_ref,
     pairs_ref, out_ref, tok_v, w_v, kv, q_v, neg_s, m_s, l_s, acc_s, att, wall,
-    load_sem, right_send, right_recv, left_send, left_recv,
-    att_send, att_recv, wt_send, wt_recv,
+    load_sem, left_send, right_send, side_send, core_send, col_recv, side_recv, core_recv,
+    swap_send, swap_recv, att_send, att_recv, wt_send, wt_recv,
 ):
-    heads, rows, width = q_v.shape
+    heads, rows, width = acc_s.shape
     cols = out_ref.shape[1]
-    half = n // 2
+    layers = n // 2
     seq = lax.axis_index("seq")
     mine = lax.axis_index("head")
-    pos = jnp.where(seq % 2 == 0, seq // 2, n - 1 - seq // 2)
-    right = ring_index((pos + 1) % n, n)
-    left = ring_index((pos + n - 1) % n, n)
+    layer, side = seq // 2, seq % 2
+    active = mine % 2 == layer % 2
+    near = mine + 1 - 2 * (mine % 2)
+    far = (mine + 2) % groups
+    other_layer = layer + 1 - 2 * (layer % 2)
+    swap_seq = other_layer * 2 + side
+    turn = jnp.where(active, 0, 1)
 
     tok_load = pltpu.make_async_copy(tok_ref, tok_v, load_sem.at[0])
     tok_load.start()
@@ -54,25 +54,63 @@
     own_cols = pl.ds(pl.multiple_of(mine * cols, LANES), cols)
     own_load = pltpu.make_async_copy(wout_ref.at[:, :, own_cols], wall.at[:, mine], load_sem.at[4])
     barrier = pltpu.get_barrier_semaphore()
-    for neighbour in (left, right):
-        pl.semaphore_signal(barrier, inc=1, device_id={"seq": neighbour}, device_id_type=MESH)
+    met = 1 + groups
+    for step in (-2, -1, 1, 2):
+        reached = (layer + step >= 0) & (layer + step < layers)
+        met = met + jnp.where(reached, 1, 0)
+
+        @pl.when(reached)
+        def _():
+            pl.semaphore_signal(
+                barrier, inc=1, device_id={"seq": seq + 2 * step}, device_id_type=MESH
+            )
+
+    pl.semaphore_signal(
+        barrier, inc=1, device_id={"seq": layer * 2 + 1 - side}, device_id_type=MESH
+    )
+    pl.semaphore_signal(
+        barrier, inc=1, device_id={"seq": swap_seq, "head": near}, device_id_type=MESH
+    )
     for offset in range(1, groups):
         pl.semaphore_signal(
             barrier, inc=1, device_id={"head": (mine + offset) % groups}, device_id_type=MESH
         )
 
-    def rightward(slot, h, hop, low, size):
-        part = kv.at[slot, h, pl.ds(low, size)]
+    def send(source, slot, h, part, send_sem, recv_sem, device):
+        low, size = part
         return pltpu.make_async_remote_copy(
-            src_ref=part, dst_ref=part, send_sem=right_send.at[hop, h],
-            recv_sem=right_recv.at[hop, h], device_id={"seq": right}, device_id_type=MESH,
-        )
-
-    def leftward(slot, h, hop, low, size):
-        part = kv.at[slot, h, pl.ds(low, size)]
+            src_ref=kv.at[source, h, pl.ds(low, size)], dst_ref=kv.at[slot, h, pl.ds(low, size)],
+            send_sem=send_sem, recv_sem=recv_sem, device_id=device, device_id_type=MESH,
+        )
+
+    def column(source, j, h, part, step):
+        sems = left_send if step < 0 else right_send
+        return send(
+            source, j * 2 + side, h, part, sems.at[j, h], col_recv.at[j, h],
+            {"seq": seq + 2 * step},
+        )
+
+    def across(source, j, h, part):
+        return send(
+            source, j * 2 + side, h, part, side_send.at[j, h], side_recv.at[j, h],
+            {"seq": layer * 2 + 1 - side},
+        )
+
+    def to_core(source, slot, h, part):
+        return send(
+            source, slot, h, part, core_send.at[slot, h], core_recv.at[slot, h], {"head": near}
+        )
+
+    def swap_copy(kind, h):
+        source, target = (
+            (q_v.at[0, h], q_v.at[1, h]),
+            (neg_s.at[0, h], neg_s.at[1, h]),
+            (q_v.at[0, h], att.at[h, near]),
+        )[kind]
         return pltpu.make_async_remote_copy(
-            src_ref=part, dst_ref=part, send_sem=left_send.at[hop, h],
-            recv_sem=left_recv.at[hop, h], device_id={"seq": left}, device_id_type=MESH,
+            src_ref=source, dst_ref=target,
+            send_sem=swap_send.at[kind, h], recv_sem=swap_recv.at[kind, h],
+            device_id={"seq": swap_seq, "head": near}, device_id_type=MESH,
         )
 
     full = (0, 2 * rows + INFO)
@@ -88,9 +126,6 @@
             device_id={"head": peer}, device_id_type=MESH,
         )
 
-    near = mine + 1 - 2 * (mine % 2)
-    far = (mine + 2) % groups
-
     def att_copy(kind, h):
         block = far if kind == 2 else mine
         return pltpu.make_async_remote_copy(
@@ -103,7 +138,7 @@
         placed = look_up(kc_ref[h], kslot_ref, h).astype(jnp.float32)
         lines = [placed[:, r * LANES : (r + 1) * LANES] for r in range(rows // LANES)]
         lines.append(jnp.zeros((INFO - rows // LANES, LANES), jnp.float32))
-        kv[pos, h, pl.ds(2 * rows, INFO)] = jnp.concatenate(lines, axis=0).astype(jnp.bfloat16)
+        kv[n, h, pl.ds(2 * rows, INFO)] = jnp.concatenate(lines, axis=0).astype(jnp.bfloat16)
 
     tok_load.wait()
     w_loads[1].wait()
@@ -111,21 +146,36 @@
     w_loads[0].start()
     keys = jnp.dot(tok_v[...], w_v[1], preferred_element_type=jnp.float32)
     for h in range(heads):
-        kv[pos, h, pl.ds(rows, rows)] = normalize(
+        kv[n, h, pl.ds(rows, rows)] = normalize(
             keys[:, h * width : (h + 1) * width], kg_ref[...]
         ).astype(jnp.bfloat16)
-    pl.semaphore_wait(barrier, 1 + groups)
-    for h in range(heads):
-        rightward(pos, h, 0, *key_part).start()
-        leftward(pos, h, 0, *key_part).start()
+    can_left = {step: layer - step >= 0 for step in (1, 2)}
+    can_right = {step: layer + step < layers for step in (1, 2)}
+
+    def each_own(part, action):
+        for step in (1, 2):
+            wanted = active if step == 2 else jnp.logical_not(active)
+            for direction, allowed in ((-step, can_left[step]), (step, can_right[step])):
+
+                @pl.when(wanted & allowed)
+                def _():
+                    for h in range(heads):
+                        action(column(n, layer, h, part, direction))
+
+        @pl.when(active)
+        def _():
+            for h in range(heads):
+                action(across(n, layer, h, part))
+                action(to_core(n, seq, h, part))
+
+    pl.semaphore_wait(barrier, met)
+    each_own(key_part, lambda copy: copy.start())
     w_loads[2].wait()
     values = jnp.dot(tok_v[...], w_v[2], preferred_element_type=jnp.float32)
     for h in range(heads):
-        kv[pos, h, pl.ds(0, rows)] = values[:, h * width : (h + 1) * width].astype(jnp.bfloat16)
-
-    for h in range(heads):
-        rightward(pos, h, 0, *value_part).start()
-        leftward(pos, h, 0, *value_part).start()
+        kv[n, h, pl.ds(0, rows)] = values[:, h * width : (h + 1) * width].astype(jnp.bfloat16)
+
+    each_own(value_part, lambda copy: copy.start())
     own_load.start()
     for offset in range(1, groups):
         weights_copy(offset).start()
@@ -133,11 +183,11 @@
     w_loads[0].wait()
     queries = jnp.dot(tok_v[...], w_v[0], preferred_element_type=jnp.float32)
     for h in range(heads):
-        q_v[h] = normalize(queries[:, h * width : (h + 1) * width], qg_ref[...]).astype(
+        q_v[0, h] = normalize(queries[:, h * width : (h + 1) * width], qg_ref[...]).astype(
             jnp.bfloat16
         )
     members, lists = pairs_ref.shape[1:]
-    slots = neg_s.shape[2]
+    slots = neg_s.shape[3]
     padded = -(-members // LANES) * LANES
     member_ids = lax.broadcasted_iota(jnp.int32, (padded, rows), 0)
     slot_ids = lax.broadcasted_iota(jnp.int32, (members, slots), 1)
@@ -152,7 +202,14 @@
             blank = jnp.zeros((padded - members, slots), jnp.float32)
             listed = jnp.concatenate([listed, blank], axis=0)
         allowed = jnp.dot(owned, listed.astype(jnp.bfloat16), preferred_element_type=jnp.float32)
-        neg_s[h] = jnp.where(allowed > 0.5, 0.0, NEG).astype(jnp.bfloat16)
+        neg_s[0, h] = jnp.where(allowed > 0.5, 0.0, NEG).astype(jnp.bfloat16)
+
+    @pl.when(jnp.logical_not(active))
+    def _():
+        for h in range(heads):
+            swap_copy(0, h).start()
+            swap_copy(1, h).start()
+
     m_s[...] = jnp.full(m_s.shape, START, jnp.float32)
     l_s[...] = jnp.zeros(l_s.shape, jnp.float32)
     acc_s[...] = jnp.zeros(acc_s.shape, jnp.float32)
@@ -166,8 +223,8 @@
         ids = lax.broadcasted_iota(jnp.int32, (slots, rows), 0).astype(jnp.float32)
         owner = jnp.where(ids == row, 1.0, 0.0).astype(jnp.bfloat16)
         scores = lax.dot_general(
-            q_v[h], block_keys, (((1,), (1,)), ((), ())), preferred_element_type=jnp.float32
-        ) + jnp.dot(neg_s[h], owner, preferred_element_type=jnp.float32)
+            q_v[turn, h], block_keys, (((1,), (1,)), ((), ())), preferred_element_type=jnp.float32
+        ) + jnp.dot(neg_s[turn, h], owner, preferred_element_type=jnp.float32)
         before = m_s[h][:, :1]
         highest = jnp.maximum(before, jnp.max(scores, axis=1, keepdims=True))
         weights = jnp.exp2((scores - highest) * factor)
@@ -183,31 +240,90 @@
     def each_head(action):
         lax.fori_loop(0, heads, lambda h, c: (action(h), c)[1], 0)
 
-    each_head(lambda h: attend(pos, h))
-
-    def passing(hop, right_next, left_next):
-        from_left = (pos + n - hop) % n
-        from_right = (pos + hop) % n
-
-        def forward(h):
-            rightward(from_left, h, hop - 1, *full).wait_recv()
-            rightward(from_left, h, hop, *right_next).start()
-            leftward(from_right, h, hop - 1, *full).wait_recv()
-            leftward(from_right, h, hop, *left_next).start()
-            attend(from_left, h)
-            attend(from_right, h)
-
-        each_head(forward)
-
-    lax.fori_loop(1, half - 1, lambda hop, c: (passing(hop, full, full), c)[1], 0)
-    passing(half - 1, key_part, value_part)
-
-    opposite = (pos + half) % n
-    for h in range(heads):
-        rightward(opposite, h, half - 1, *key_part).wait_recv()
-        leftward(opposite, h, half - 1, *value_part).wait_recv()
-        attend(opposite, h)
-        att[h, mine] = (acc_s[h] / jnp.maximum(l_s[h], 1.0)).astype(jnp.bfloat16)
+    def when_layer(j, action):
+        pl.when((j >= 0) & (j < layers))(lambda: action(j))
+
+    def each_forward(j, h, action):
+        slot = j * 2 + side
+        action(across(slot, j, h, full))
+        action(to_core(slot, slot, h, full))
+        pl.when((j > layer) & can_left[2])(lambda: action(column(slot, j, h, full, -2)))
+        pl.when((j < layer) & can_right[2])(lambda: action(column(slot, j, h, full, 2)))
+
+    def column_event(j):
+        def one(h):
+            column(n, j, h, full, 0).wait_recv()
+            each_forward(j, h, lambda copy: copy.start())
+            attend(j * 2 + side, h)
+
+        each_head(one)
+
+    def side_event(j):
+        slot = j * 2 + 1 - side
+
+        def one(h):
+            send(n, slot, h, full, side_send.at[j, h], side_recv.at[j, h], {"head": near}).wait_recv()
+            to_core(slot, slot, h, full).start()
+            attend(slot, h)
+
+        each_head(one)
+
+    def core_event(slot):
+        def one(h):
+            to_core(n, slot, h, full).wait_recv()
+            attend(slot, h)
+
+        each_head(one)
+
+    def at_distance(d, action):
+        def one(i, carry):
+            when_layer(layer + d * (1 - 2 * i), action)
+            return carry
+
+        lax.fori_loop(0, jnp.where(d == 0, 1, 2), one, 0)
+
+    def by_distance(column_action, side_action):
+        def one(d, carry):
+            at_distance(d, column_action)
+            at_distance(d - 1, side_action)
+            return carry
+
+        lax.fori_loop(1, layers, one, 0)
+        at_distance(jnp.int32(layers - 1), side_action)
+
+    @pl.when(active)
+    def _():
+        each_head(lambda h: attend(n, h))
+        by_distance(column_event, side_event)
+
+    @pl.when(jnp.logical_not(active))
+    def _():
+        for h in range(heads):
+            swap_copy(0, h).wait_recv()
+            swap_copy(1, h).wait_recv()
+        core_event(seq)
+        by_distance(
+            lambda j: core_event(j * 2 + side), lambda j: core_event(j * 2 + 1 - side)
+        )
+        for h in range(heads):
+            swap_copy(0, h).wait_send()
+            q_v[0, h] = (acc_s[h] / jnp.maximum(l_s[h], 1.0)).astype(jnp.bfloat16)
+            swap_copy(2, h).start()
+
+    for h in range(heads):
+        @pl.when(active)
+        def _():
+            att[h, mine] = (acc_s[h] / jnp.maximum(l_s[h], 1.0)).astype(jnp.bfloat16)
+
+        @pl.when(jnp.logical_not(active))
+        def _():
+            att_in = pltpu.make_async_remote_copy(
+                src_ref=q_v.at[0, h], dst_ref=att.at[h, mine],
+                send_sem=swap_send.at[2, h], recv_sem=swap_recv.at[2, h],
+                device_id={"seq": swap_seq, "head": near}, device_id_type=MESH,
+            )
+            att_in.wait_recv()
+
         att_copy(0, h).start()
         att_copy(1, h).start()
         if h > 0:
@@ -237,17 +353,24 @@
         for kind in range(3):
             att_copy(kind, h).wait_send()
 
-    def drain(hop):
-        def one(h):
-            rightward(pos, h, hop, *full).wait_send()
-            leftward(pos, h, hop, *full).wait_send()
-
-        each_head(one)
-
-    lax.fori_loop(0, half - 1, lambda hop, c: (drain(hop), c)[1], 0)
-    for h in range(heads):
-        rightward(pos, h, half - 1, *key_part).wait_send()
-        leftward(pos, h, half - 1, *value_part).wait_send()
+    each_own(full, lambda copy: copy.wait_send())
+
+    @pl.when(active)
+    def _():
+        def column_drain(j):
+            each_head(lambda h: each_forward(j, h, lambda copy: copy.wait_send()))
+
+        def side_drain(j):
+            slot = j * 2 + 1 - side
+            each_head(lambda h: to_core(slot, slot, h, full).wait_send())
+
+        by_distance(column_drain, side_drain)
+
+    @pl.when(jnp.logical_not(active))
+    def _():
+        for h in range(heads):
+            swap_copy(1, h).wait_send()
+            swap_copy(2, h).wait_send()
 
 
 def body(
@@ -276,9 +399,9 @@
         scratch_shapes=[
             pltpu.VMEM((rows, depth), bf16),
             pltpu.VMEM((3, depth, heads * width), bf16),
-            pltpu.VMEM((n, heads, 2 * rows + INFO, width), bf16),
-            pltpu.VMEM((heads, rows, width), bf16),
-            pltpu.VMEM((heads, rows, slots), bf16),
+            pltpu.VMEM((n + 1, heads, 2 * rows + INFO, width), bf16),
+            pltpu.VMEM((2, heads, rows, width), bf16),
+            pltpu.VMEM((2, heads, rows, slots), bf16),
             pltpu.VMEM((heads, rows, width), jnp.float32),
             pltpu.VMEM((heads, rows, width), jnp.float32),
             pltpu.VMEM((heads, rows, width), jnp.float32),
@@ -288,7 +411,12 @@
             dma((n // 2, heads)),
             dma((n // 2, heads)),
             dma((n // 2, heads)),
+            dma((n, heads)),
             dma((n // 2, heads)),
+            dma((n // 2, heads)),
+            dma((n, heads)),
+            dma((3, heads)),
+            dma((3, heads)),
             dma((3, heads)),
             dma((3, heads)),
             dma((groups,)),

time: 49.2 us -> 48.2 us (0.980)
  Pallas kernels: 46.8 us -> 46.2 us
    pallas_call x1, Pallas kernels: 46.8 us -> 46.2 us  [body(): pl.pallas_call(functools.partial(kernel, n, groups), out_shape=jax.ShapeD...]
where the time goes in v4:
time: 48.2 us; the launch traced here: 48 us
  Pallas kernels  46.2 us (96%)
  local copies, waits for them, and re-layouts  1.77 us (4%)
    pallas_call x1, Pallas kernels, body(): pl.pallas_call(functools.partial(kernel, n, groups), out_shape=jax.ShapeD...  46.2 us
    unnamed x1, local copies, waits for them, and re-layouts  1.77 us

profile of v4, /device:TPU:0, one launch (start us, length us, event | category | flops | bytes accessed | tf_op | source)
XLA Modules:
  0.0 48.0 jit_solution(5635590350739817593)
XLA Ops:
  0.0 46.2 %shard_map.100 = bf16[256,768]{1,0:T(8,128)(2,1)} custom-call(bf16[256,3072]{1,0:T(8,128)(2,1)} %tok_ref.1, bf16[3,3072,384]{2,1,0:T(8,128)(2,1)} %bitcast.6, f32[1,128]{1,0:T(1,128)} %bitcast.10, f32[1,128]{1,0:T(1,128)} %bitcast.11, bf16[3,128,3072]{2,1,0:T(8,128)(2,1)} %bitcast.7, s32[3,1,256]{2,1,0:T(1,128)} %bitcast.8, s32[3,1,256]{2,1,0:T(1,128)} %bitcast.9, ...), custom_call_target="tpu_custom_call" | custom-call | flops 2415919104 | bytes 12582912 | tf_op jit(solution)/shard_map/pallas_call | solution.py:394
  46.2 1.8 %copy.12 = bf16[256,768]{1,0:T(8,128)(2,1)} copy(bf16[256,768]{1,0:T(8,128)(2,1)} %shard_map.100) | data formatting | bytes 786432

commit v5 on v4

--- a/solution.py
+++ b/solution.py
@@ -258,22 +258,36 @@
 
         each_head(one)
 
+    def side_piece(j, h):
+        slot = j * 2 + 1 - side
+        send(n, slot, h, full, side_send.at[j, h], side_recv.at[j, h], {"head": near}).wait_recv()
+        to_core(slot, slot, h, full).start()
+        attend(slot, h)
+
     def side_event(j):
-        slot = j * 2 + 1 - side
-
-        def one(h):
-            send(n, slot, h, full, side_send.at[j, h], side_recv.at[j, h], {"head": near}).wait_recv()
-            to_core(slot, slot, h, full).start()
-            attend(slot, h)
-
-        each_head(one)
+        each_head(lambda h: side_piece(j, h))
+
+    def core_piece(slot, h):
+        to_core(n, slot, h, full).wait_recv()
+        attend(slot, h)
 
     def core_event(slot):
-        def one(h):
-            to_core(n, slot, h, full).wait_recv()
-            attend(slot, h)
-
-        each_head(one)
+        each_head(lambda h: core_piece(slot, h))
+
+    farthest = jnp.where(layer * 2 < layers, layers - 1, 0)
+
+    def but_last(action):
+        return lambda j: pl.when(j != farthest)(lambda: action(j))
+
+    def share(h):
+        att_copy(0, h).start()
+        att_copy(1, h).start()
+        if h > 0:
+            att_copy(1, h - 1).wait_recv()
+            att_copy(2, h - 1).start()
+
+    def attended(h):
+        return (acc_s[h] / jnp.maximum(l_s[h], 1.0)).astype(jnp.bfloat16)
 
     def at_distance(d, action):
         def one(i, carry):
@@ -294,7 +308,11 @@
     @pl.when(active)
     def _():
         each_head(lambda h: attend(n, h))
-        by_distance(column_event, side_event)
+        by_distance(column_event, but_last(side_event))
+        for h in range(heads):
+            side_piece(farthest, h)
+            att[h, mine] = attended(h)
+            share(h)
 
     @pl.when(jnp.logical_not(active))
     def _():
@@ -303,32 +321,21 @@
             swap_copy(1, h).wait_recv()
         core_event(seq)
         by_distance(
-            lambda j: core_event(j * 2 + side), lambda j: core_event(j * 2 + 1 - side)
-        )
-        for h in range(heads):
+            lambda j: core_event(j * 2 + side), but_last(lambda j: core_event(j * 2 + 1 - side))
+        )
+        for h in range(heads):
+            core_piece(farthest * 2 + 1 - side, h)
             swap_copy(0, h).wait_send()
-            q_v[0, h] = (acc_s[h] / jnp.maximum(l_s[h], 1.0)).astype(jnp.bfloat16)
+            q_v[0, h] = attended(h)
             swap_copy(2, h).start()
-
-    for h in range(heads):
-        @pl.when(active)
-        def _():
-            att[h, mine] = (acc_s[h] / jnp.maximum(l_s[h], 1.0)).astype(jnp.bfloat16)
-
-        @pl.when(jnp.logical_not(active))
-        def _():
-            att_in = pltpu.make_async_remote_copy(
+        for h in range(heads):
+            returned = pltpu.make_async_remote_copy(
                 src_ref=q_v.at[0, h], dst_ref=att.at[h, mine],
                 send_sem=swap_send.at[2, h], recv_sem=swap_recv.at[2, h],
                 device_id={"seq": swap_seq, "head": near}, device_id_type=MESH,
             )
-            att_in.wait_recv()
-
-        att_copy(0, h).start()
-        att_copy(1, h).start()
-        if h > 0:
-            att_copy(1, h - 1).wait_recv()
-            att_copy(2, h - 1).start()
+            returned.wait_recv()
+            share(h)
 
     own_load.wait()
     for offset in range(1, groups):

time: 48.2 us -> 48.6 us (level)
  no operation moved by 1% of the time
where the time goes in v5:
time: 48.6 us; the launch traced here: 48.2 us
  Pallas kernels  46.4 us (95%)
  local copies, waits for them, and re-layouts  1.77 us (4%)
    pallas_call x1, Pallas kernels, body(): pl.pallas_call(functools.partial(kernel, n, groups), out_shape=jax.ShapeD...  46.4 us
    unnamed x1, local copies, waits for them, and re-layouts  1.77 us

profile of v5, /device:TPU:0, one launch (start us, length us, event | category | flops | bytes accessed | tf_op | source)
XLA Modules:
  0.0 48.2 jit_solution(13455578654036549913)
XLA Ops:
  0.0 46.4 %shard_map.100 = bf16[256,768]{1,0:T(8,128)(2,1)} custom-call(bf16[256,3072]{1,0:T(8,128)(2,1)} %tok_ref.1, bf16[3,3072,384]{2,1,0:T(8,128)(2,1)} %bitcast.6, f32[1,128]{1,0:T(1,128)} %bitcast.10, f32[1,128]{1,0:T(1,128)} %bitcast.11, bf16[3,128,3072]{2,1,0:T(8,128)(2,1)} %bitcast.7, s32[3,1,256]{2,1,0:T(1,128)} %bitcast.8, s32[3,1,256]{2,1,0:T(1,128)} %bitcast.9, ...), custom_call_target="tpu_custom_call" | custom-call | flops 2415919104 | bytes 12582912 | tf_op jit(solution)/shard_map/pallas_call | solution.py:401
  46.4 1.8 %copy.12 = bf16[256,768]{1,0:T(8,128)(2,1)} copy(bf16[256,768]{1,0:T(8,128)(2,1)} %shard_map.100) | data formatting | bytes 786432

commit v6 on v4

--- a/solution.py
+++ b/solution.py
@@ -170,6 +170,8 @@
 
     pl.semaphore_wait(barrier, met)
     each_own(key_part, lambda copy: copy.start())
+    for offset in range(1, groups):
+        weights_copy(offset).start()
     w_loads[2].wait()
     values = jnp.dot(tok_v[...], w_v[2], preferred_element_type=jnp.float32)
     for h in range(heads):
@@ -177,8 +179,6 @@
 
     each_own(value_part, lambda copy: copy.start())
     own_load.start()
-    for offset in range(1, groups):
-        weights_copy(offset).start()
 
     w_loads[0].wait()
     queries = jnp.dot(tok_v[...], w_v[0], preferred_element_type=jnp.float32)
@@ -245,10 +245,10 @@
 
     def each_forward(j, h, action):
         slot = j * 2 + side
+        pl.when((j > layer) & can_left[2])(lambda: action(column(slot, j, h, full, -2)))
+        pl.when((j < layer) & can_right[2])(lambda: action(column(slot, j, h, full, 2)))
         action(across(slot, j, h, full))
         action(to_core(slot, slot, h, full))
-        pl.when((j > layer) & can_left[2])(lambda: action(column(slot, j, h, full, -2)))
-        pl.when((j < layer) & can_right[2])(lambda: action(column(slot, j, h, full, 2)))
 
     def column_event(j):
         def one(h):

time: 48.2 us -> 48.2 us (level)
  no operation moved by 1% of the time
where the time goes in v6:
time: 48.2 us; the launch traced here: 47.9 us
  Pallas kernels  46.2 us (96%)
  local copies, waits for them, and re-layouts  1.77 us (4%)
    pallas_call x1, Pallas kernels, body(): pl.pallas_call(functools.partial(kernel, n, groups), out_shape=jax.ShapeD...  46.2 us
    unnamed x1, local copies, waits for them, and re-layouts  1.77 us

profile of v6, /device:TPU:0, one launch (start us, length us, event | category | flops | bytes accessed | tf_op | source)
XLA Modules:
  0.0 47.9 jit_solution(5252325867386973954)
XLA Ops:
  0.0 46.2 %shard_map.100 = bf16[256,768]{1,0:T(8,128)(2,1)} custom-call(bf16[256,3072]{1,0:T(8,128)(2,1)} %tok_ref.1, bf16[3,3072,384]{2,1,0:T(8,128)(2,1)} %bitcast.6, f32[1,128]{1,0:T(1,128)} %bitcast.10, f32[1,128]{1,0:T(1,128)} %bitcast.11, bf16[3,128,3072]{2,1,0:T(8,128)(2,1)} %bitcast.7, s32[3,1,256]{2,1,0:T(1,128)} %bitcast.8, s32[3,1,256]{2,1,0:T(1,128)} %bitcast.9, ...), custom_call_target="tpu_custom_call" | custom-call | flops 2415919104 | bytes 12582912 | tf_op jit(solution)/shard_map/pallas_call | solution.py:394
  46.2 1.8 %copy.12 = bf16[256,768]{1,0:T(8,128)(2,1)} copy(bf16[256,768]{1,0:T(8,128)(2,1)} %shard_map.100) | data formatting | bytes 786432
